TPU v7x, 512 devices: a whole 4x8x8 slice. The times are simulated.
512 devices in a mesh: field: 32 (over x, y), cap: 4 (over z_lo, core), bank: 4 (over z_hi).
Axes of the slice: x: 4, y: 8, z: 8 (z_hi: 4, z_lo: 2; z = z_hi * 2 + z_lo), core: 2. Of those that a mesh axis runs over, the one named last changes fastest.
Arguments:
- pattern: bfloat16 [4, 3, 542, 8192], P('cap', None, None, 'field'), may hold values from -6 to 6
- measured: bfloat16 [4, 3, 32, 8192], P('cap', None, None, 'field'), may hold values from -6 to 6
- row_kernels: bfloat16 [64, 3, 16, 511], P('field', None, 'bank'), may hold values from -0.125 to 0.125
- col_kernels: bfloat16 [64, 3, 16, 511], P('field', None, 'bank'), may hold values from -0.125 to 0.125
- tile_patch: int32 [64], P('field'), may hold values from 0 to 1
- sat_tiles: int32 [4, 256], P('cap'), may hold values from 0 to 1023
Outputs:
- grad_rows: float32 [64, 3, 16, 511], P('field', None, 'bank')
- grad_cols: float32 [64, 3, 16, 511], P('field', None, 'bank')
Inputs may be any that keep to these rules, and one draw needn't show every extreme that they name: Patch t of the window uses kernel set (t // 2) * 2 + tile_patch[t]. `sat_tiles`: tile numbers run row by row over tiles of 16 x 16 pixels of the window; an entry may repeat.
All inputs are finite; a program needn't handle non-finite values.
Results may differ from a plain program's by a relative error of at most 0.0033.
Values may be sent and summed in bfloat16 or wider, within the bound.
A program may use at most 64 MiB of HBM per device.

v0:
```python
import jax
import jax.numpy as jnp
from jax import lax
from jax.sharding import PartitionSpec as P

TILE = 16


def with_halo(cells, sides, width):
    for axis, dim in sides:
        count = lax.axis_size(axis)
        ends = count - 1
        head = lax.slice_in_dim(cells, 0, width, axis=dim)
        tail = lax.slice_in_dim(cells, cells.shape[dim] - width, cells.shape[dim], axis=dim)
        cells = jnp.concatenate(
            [
                lax.ppermute(tail, axis, [(i, (i + 1) % count) for i in range(ends)]),
                cells,
                lax.ppermute(head, axis, [((i + 1) % count, i) for i in range(ends)]),
            ],
            axis=dim,
        )
    return cells


def banded(kernel, band_width):
    tap_count = kernel.shape[-1]
    span_len = band_width + tap_count - 1
    zero_tail = jnp.zeros(kernel.shape[:-1] + (band_width,), kernel.dtype)
    padded = jnp.concatenate([kernel, zero_tail], axis=-1)
    repeated = jnp.tile(padded, (1,) * (kernel.ndim - 1) + (band_width,))
    return repeated[..., : band_width * span_len].reshape(
        kernel.shape[:-1] + (band_width, span_len)
    )


def diagonals(matrix, tap_count):
    line_count = matrix.shape[-2]
    span_len = matrix.shape[-1]
    flattened = matrix.reshape(matrix.shape[:-2] + (line_count * span_len,))
    lead_len = (line_count - 1) * (span_len + 1)
    shaped = flattened[..., :lead_len].reshape(matrix.shape[:-2] + (line_count - 1, span_len + 1))
    last_line = flattened[..., lead_len : lead_len + tap_count]
    return jnp.sum(shaped[..., :tap_count], axis=-2) + last_line


def body(pattern, measured, row_kernels, col_kernels, tile_patch, sat_tiles):
    captures, colours, rows_ext, strip_width = pattern.shape
    height = measured.shape[2]
    tap_count = row_kernels.shape[-1]
    rim_width = (tap_count - 1) // 2
    tile_count = row_kernels.shape[0]
    patch_width = strip_width // tile_count
    extended = with_halo(pattern, (("field", 3),), rim_width)
    strip_tiles = strip_width // TILE
    across = strip_tiles * lax.axis_size("field")
    row_ids = jnp.arange(height // TILE, dtype=jnp.int32)
    col_ids = lax.axis_index("field") * strip_tiles + jnp.arange(strip_tiles, dtype=jnp.int32)
    tile_ids = row_ids[:, None] * across + col_ids[None, :]
    saturated = jnp.any(tile_ids[None, :, :, None] == sat_tiles[:, None, None, :], axis=-1)
    keep_tiles = 1.0 - saturated.astype(jnp.float32)
    keep_pixels = jnp.broadcast_to(
        keep_tiles[:, :, None, :, None], (captures, height // TILE, TILE, strip_tiles, TILE)
    ).reshape(captures, height, strip_width)
    slots = jnp.arange(tile_count, dtype=jnp.int32)
    selectors = []
    windows = []
    col_bands = []
    rowpasses = []
    partials = []
    for tile_index in range(tile_count):
        selector = (tile_patch[tile_index] == slots).astype(jnp.float32)
        row_taps = jnp.einsum("k,kqrb->qrb", selector, row_kernels.astype(jnp.float32)).astype(
            jnp.bfloat16
        )
        col_taps = jnp.einsum("k,kqrb->qrb", selector, col_kernels.astype(jnp.float32)).astype(
            jnp.bfloat16
        )
        row_band = banded(row_taps, patch_width)
        col_band = banded(col_taps, height)
        start = tile_index * patch_width
        window_cols = extended[..., start : start + patch_width + 2 * rim_width]
        rowpass = jnp.einsum(
            "cqyj,qrxj->cqryx", window_cols, row_band, preferred_element_type=jnp.float32
        ).astype(jnp.bfloat16)
        partial_tile = jnp.einsum(
            "qryk,cqrkx->cqyx", col_band, rowpass, preferred_element_type=jnp.float32
        )
        selectors.append(selector)
        windows.append(window_cols)
        col_bands.append(col_band)
        rowpasses.append(rowpass)
        partials.append(partial_tile)
    partial_value = jnp.concatenate(partials, axis=3)
    predicted = lax.psum(partial_value, "bank")
    residual = (keep_pixels[:, None] * (predicted - measured.astype(jnp.float32))).astype(
        jnp.bfloat16
    )
    rank_count = row_kernels.shape[2]
    row_total = jnp.zeros((tile_count, colours, rank_count, tap_count), jnp.float32)
    col_total = jnp.zeros((tile_count, colours, rank_count, tap_count), jnp.float32)
    for tile_index in range(tile_count):
        start = tile_index * patch_width
        residual_tile = residual[..., start : start + patch_width]
        backward = jnp.einsum(
            "qryk,cqyx->cqrkx",
            col_bands[tile_index],
            residual_tile,
            preferred_element_type=jnp.float32,
        ).astype(jnp.bfloat16)
        row_terms = jnp.einsum(
            "cqrkx,cqkj->qrxj", backward, windows[tile_index], preferred_element_type=jnp.float32
        )
        col_terms = jnp.einsum(
            "cqyx,cqrkx->qryk",
            residual_tile,
            rowpasses[tile_index],
            preferred_element_type=jnp.float32,
        )
        row_grad = diagonals(row_terms, tap_count)
        col_grad = diagonals(col_terms, tap_count)
        row_total = row_total + selectors[tile_index][:, None, None, None] * row_grad[None]
        col_total = col_total + selectors[tile_index][:, None, None, None] * col_grad[None]
    summed_rows, summed_cols = lax.psum((row_total, col_total), "cap")
    return (summed_rows * (1.0 / height), summed_cols * (1.0 / height))


def solution(mesh):
    return jax.shard_map(
        body,
        mesh=mesh,
        in_specs=(
            P("cap", None, None, "field"),
            P("cap", None, None, "field"),
            P("field", None, "bank", None),
            P("field", None, "bank", None),
            P("field"),
            P("cap", None),
        ),
        out_specs=(P("field", None, "bank", None), P("field", None, "bank", None)),
        check_vma=False,
    )
```

profile of v0, /device:TPU:1, one launch (start us, length us, event | category | flops | bytes accessed | tf_op | source)
XLA Modules:
  0.0 245.0 jit_solution(10084475282999751488)
XLA Ops:
  7.3 3.0 %fusion.46 = (bf16[1,3,542,255]{3,2,1,0:T(8,128)(2,1)}, bf16[1,3,542,255]{3,2,1,0:T(8,128)(2,1)}) fusion(bf16[1,3,542,256]{3,2,1,0:T(8,128)(2,1)} %param.6), kind=kLoop, calls=%fused_computation.70 | loop fusion | bytes 3317040 | tf_op jit(solution)/shard_map/slice | solution.py:14
  10.2 4.9 %collective-permute-start = (bf16[1,3,542,255]{3,2,1,0:T(8,128)(2,1)}, bf16[1,3,542,255]{3,2,1,0:T(8,128)(2,1)}, u32[]{:S(2)}, u32[]{:S(2)}) collective-permute-start(bf16[1,3,542,255]{3,2,1,0:T(8,128)(2,1)} %get-tuple-element.4), channel_id=1, source_target_pairs={{0,16},{16,32},{32,48},{48,64},{64,80},{80,96},{96,112},{112,128},... | collective-permute-start | bytes 2487788 | tf_op jit(solution)/shard_map/ppermute | solution.py:17
  24.1 1.6 reshape.178
  25.9 5.4 %tile.41 = bf16[3,4,81792]{2,1,0:T(4,128)(2,1)} reshape(bf16[3,4,128,639]{3,2,1,0:T(8,128)(2,1)S(1)} %tile.40) | data formatting | bytes 3926016 | tf_op jit(solution)/shard_map/tile | solution.py:31
  32.9 5.2 %reshape.179 = bf16[3,4,128,638]{3,2,1,0:T(8,128)(2,1)} reshape(bf16[3,4,81664]{2,1,0:T(4,128)(2,1)S(1)} %slice-done) | data formatting | bytes 3919872 | tf_op jit(solution)/shard_map/reshape | solution.py:32
  38.2 5.3 %tile.17 = bf16[3,4,81792]{2,1,0:T(4,128)(2,1)} reshape(bf16[3,4,128,639]{3,2,1,0:T(8,128)(2,1)S(1)} %tile.16) | data formatting | bytes 3926016 | tf_op jit(solution)/shard_map/tile | solution.py:31
  45.0 5.2 %reshape.175 = bf16[3,4,128,638]{3,2,1,0:T(8,128)(2,1)} reshape(bf16[3,4,81664]{2,1,0:T(4,128)(2,1)S(1)} %slice-done.1) | data formatting | bytes 3919872 | tf_op jit(solution)/shard_map/reshape | solution.py:32
  50.3 2.7 %pad_maximum_fusion = bf16[1,3,542,766]{3,2,1,0:T(8,128)(2,1)S(1)} fusion(bf16[1,3,542,255]{3,2,1,0:T(8,128)(2,1)} %collective-permute-done.1, bf16[1,3,542,256]{3,2,1,0:T(8,128)(2,1)S(1)} %copy-done.2, bf16[1,3,542,255]{3,2,1,0:T(8,128)(2,1)} %collective-permute-done), kind=kLoop, calls=%fused_computation.2 | loop fusion | flops 7473096 | bytes 4982064 | tf_op jit(solution)/shard_map/concatenate | solution.py:15
  60.6 58.8 %all-reduce.8.cloned.1.call-done = f32[1,3,32,256]{3,2,1,0:T(8,128)} async-done(((f32[1,3,32,256]{3,2,1,0:T(8,128)}), f32[1,3,32,256]{3,2,1,0:T(8,128)}) %all-reduce.8.cloned.1.call-update) | async-done | bytes 98320 | tf_op jit(solution)/shard_map/psum | solution.py:95
  120.3 1.7 fusion.19
  122.0 1.7 fusion.16
  123.7 6.2 %fusion.2 = f32[3,4,128,638]{3,2,1,0:T(8,128)} fusion(bf16[1,3,542,766]{3,2,1,0:T(8,128)(2,1)} %copy-done.5, bf16[3,4,32,542]{3,2,1,0:T(8,128)(2,1)S(1)} %copy-done.9, bf16[1,3,32,256]{3,2,1,0:T(8,128)(2,1)S(1)} %multiply_convert_fusion), kind=kOutput, calls=%fused_computation.7 | convolution fusion | flops 1116398592 | bytes 6524928 | tf_op jit(solution)/shard_map/cqrkx,cqkj->qrxj/dot_general | solution.py:111
  129.9 6.3 %fusion = f32[3,4,128,638]{3,2,1,0:T(8,128)} fusion(bf16[1,3,542,766]{3,2,1,0:T(8,128)(2,1)} %copy-done.5, bf16[3,4,32,542]{3,2,1,0:T(8,128)(2,1)S(1)} %copy-done.11, bf16[1,3,32,256]{3,2,1,0:T(8,128)(2,1)S(1)} %multiply_convert_fusion), kind=kOutput, calls=%fused_computation.5 | convolution fusion | flops 1116398592 | bytes 6524928 | tf_op jit(solution)/shard_map/cqrkx,cqkj->qrxj/dot_general | solution.py:111
  138.4 2.0 reshape.194
  141.7 2.0 reshape.192
  145.0 7.2 %reshape.189 = f32[3,4,81664]{2,1,0:T(4,128)} reshape(f32[3,4,128,638]{3,2,1,0:T(8,128)} %fusion.2) | data formatting | bytes 7839744 | tf_op jit(solution)/shard_map/reshape | solution.py:40
  152.2 6.9 %reshape.185 = f32[3,4,81664]{2,1,0:T(4,128)} reshape(f32[3,4,128,638]{3,2,1,0:T(8,128)} %fusion) | data formatting | bytes 7839744 | tf_op jit(solution)/shard_map/reshape | solution.py:40
  159.1 4.3 %slice.103 = f32[3,4,81153]{2,1,0:T(4,128)} slice(f32[3,4,81664]{2,1,0:T(4,128)} %reshape.185), slice={[0:3], [0:4], [0:81153]} | slice | bytes 7790688 | tf_op jit(solution)/shard_map/slice | solution.py:42
  163.4 7.3 %reshape.186 = f32[3,4,127,639]{3,2,1,0:T(8,128)} reshape(f32[3,4,81153]{2,1,0:T(4,128)} %slice.103) | data formatting | bytes 7790688 | tf_op jit(solution)/shard_map/reshape | solution.py:42
  170.6 2.3 slice_reduce_fusion.1
  172.9 4.3 %slice.107 = f32[3,4,81153]{2,1,0:T(4,128)} slice(f32[3,4,81664]{2,1,0:T(4,128)} %reshape.189), slice={[0:3], [0:4], [0:81153]} | slice | bytes 7790688 | tf_op jit(solution)/shard_map/slice | solution.py:42
  177.2 7.3 %reshape.190 = f32[3,4,127,639]{3,2,1,0:T(8,128)} reshape(f32[3,4,81153]{2,1,0:T(4,128)} %slice.107) | data formatting | bytes 7790688 | tf_op jit(solution)/shard_map/reshape | solution.py:42
  184.5 2.3 slice_reduce_fusion
  188.4 46.9 %all-reduce.10.cloned.1.call-done = (f32[2,3,4,511]{3,2,1,0:T(4,128)}, f32[2,3,4,511]{3,2,1,0:T(4,128)}) async-done(((f32[2,3,4,511]{3,2,1,0:T(4,128)}, f32[2,3,4,511]{3,2,1,0:T(4,128)}), (f32[2,3,4,511]{3,2,1,0:T(4,128)}, f32[2,3,4,511]{3,2,1,0:T(4,128)})) %all-reduce.10.cloned.1.call-update) | async-done | bytes 98128 | tf_op jit(solution)/shard_map/psum | solution.py:124
  (88 shorter events, 30.1 us)
Async XLA Ops:
  7.2 9.9 %copy-start = (bf16[2,3,4,511]{3,2,1,0:T(4,128)(2,1)S(1)}, bf16[2,3,4,511]{3,2,1,0:T(4,128)(2,1)}, u32[]{:S(2)}) copy-start(bf16[2,3,4,511]{3,2,1,0:T(4,128)(2,1)} %param.9) | copy-start | bytes 73588
  7.2 9.3 %copy-start.13 = (s32[2]{0:T(128)S(1)}, s32[2]{0:T(128)}, u32[]{:S(2)}) copy-start(s32[2]{0:T(128)} %param.10) | copy-start | bytes 28
  7.2 10.7 %copy-start.15 = (bf16[2,3,4,511]{3,2,1,0:T(4,128)(2,1)S(1)}, bf16[2,3,4,511]{3,2,1,0:T(4,128)(2,1)}, u32[]{:S(2)}) copy-start(bf16[2,3,4,511]{3,2,1,0:T(4,128)(2,1)} %param.8) | copy-start | bytes 73588
  7.2 13.3 %copy-start.14 = (s32[1,256]{1,0:T(1,128)S(1)}, s32[1,256]{1,0:T(1,128)}, u32[]{:S(2)}) copy-start(s32[1,256]{1,0:T(1,128)} %param.11) | copy-start | bytes 3076
  7.2 112.2 %all-reduce.8.cloned.1.call-start = ((), (), s32[]{:S(2)}) async-start(), calls=%async_computation | async-start | bytes 196608 | tf_op jit(solution)/shard_map/psum | solution.py:95
  10.2 40.0 %collective-permute-start = (bf16[1,3,542,255]{3,2,1,0:T(8,128)(2,1)}, bf16[1,3,542,255]{3,2,1,0:T(8,128)(2,1)}, u32[]{:S(2)}, u32[]{:S(2)}) collective-permute-start(bf16[1,3,542,255]{3,2,1,0:T(8,128)(2,1)} %get-tuple-element.4), channel_id=1, source_target_pairs={{0,16},{16,32},{32,48},{48,64},{64,80},{80,96},{96,112},{112,128},... | collective-permute-start | bytes 2487788 | tf_op jit(solution)/shard_map/ppermute | solution.py:17
  15.2 35.1 %collective-permute-start.1 = (bf16[1,3,542,255]{3,2,1,0:T(8,128)(2,1)}, bf16[1,3,542,255]{3,2,1,0:T(8,128)(2,1)}, u32[]{:S(2)}, u32[]{:S(2)}) collective-permute-start(bf16[1,3,542,255]{3,2,1,0:T(8,128)(2,1)} %get-tuple-element.5), channel_id=1, source_target_pairs={{16,0},{32,16},{48,32},{64,48},{80,64},{96,80},{112,96},{128,112},... | collective-permute-start | bytes 2487788 | tf_op jit(solution)/shard_map/ppermute | solution.py:19
  31.3 1.5 slice-start
  43.5 1.5 slice-start.1
  45.0 5.3 %copy-start.2 = (bf16[1,3,542,256]{3,2,1,0:T(8,128)(2,1)S(1)}, bf16[1,3,542,256]{3,2,1,0:T(8,128)(2,1)}, u32[]{:S(2)}) copy-start(bf16[1,3,542,256]{3,2,1,0:T(8,128)(2,1)} %param.6) | copy-start | bytes 2497540
  50.3 2.7 %copy-start.6 = (bf16[3,4,128,638]{3,2,1,0:T(8,128)(2,1)S(1)}, bf16[3,4,128,638]{3,2,1,0:T(8,128)(2,1)}, u32[]{:S(2)}) copy-start(bf16[3,4,128,638]{3,2,1,0:T(8,128)(2,1)} %reshape.179) | copy-start | bytes 5879812
  53.0 1.5 copy-start.5
  53.0 2.5 %copy-start.7 = (bf16[3,4,128,638]{3,2,1,0:T(8,128)(2,1)S(1)}, bf16[3,4,128,638]{3,2,1,0:T(8,128)(2,1)}, u32[]{:S(2)}) copy-start(bf16[3,4,128,638]{3,2,1,0:T(8,128)(2,1)} %reshape.175) | copy-start | bytes 5879812
  55.4 1.5 copy-start.8
  57.0 1.0 copy-start.10
  57.0 62.5 %copy-start.12 = (bf16[1,3,32,256]{3,2,1,0:T(8,128)(2,1)S(1)}, bf16[1,3,32,256]{3,2,1,0:T(8,128)(2,1)}, u32[]{:S(2)}) copy-start(bf16[1,3,32,256]{3,2,1,0:T(8,128)(2,1)} %param.7) | copy-start | bytes 147460
  59.1 176.3 %all-reduce.10.cloned.1.call-start = ((), (), s32[]{:S(2)}) async-start(), calls=%async_computation.1 | async-start | bytes 196608 | tf_op jit(solution)/shard_map/psum | solution.py:124
  122.0 1.7 copy-start.9
  123.7 6.2 %copy-start.11 = (bf16[3,4,32,542]{3,2,1,0:T(8,128)(2,1)S(1)}, bf16[3,4,32,542]{3,2,1,0:T(8,128)(2,1)}, u32[]{:S(2)}) copy-start(bf16[3,4,32,542]{3,2,1,0:T(8,128)(2,1)} %reshape.178) | copy-start | bytes 1248772
  129.9 6.3 %copy-start.4 = (f32[3,4,32,542]{3,2,1,0:T(8,128)S(1)}, f32[3,4,32,542]{3,2,1,0:T(8,128)}, u32[]{:S(2)}) copy-start(f32[3,4,32,542]{3,2,1,0:T(8,128)} %fusion.16) | copy-start | bytes 2497540
  136.2 1.2 copy-start.3
  177.2 61.0 %copy-start.1 = (bf16[2,3,4,511]{3,2,1,0:T(4,128)(2,1)S(1)}, bf16[2,3,4,511]{3,2,1,0:T(4,128)(2,1)}, u32[]{:S(2)}) copy-start(bf16[2,3,4,511]{3,2,1,0:T(4,128)(2,1)} %param.9) | copy-start | bytes 73588
Sparse Core Ops, SparseCore 0:
  59.2 60.1 all-reduce.7
  188.6 46.7 all-reduce.9
where the time goes:
time: 246 us; the launch traced here: 245 us
  waiting for transfers between devices  106 us (43%)
  local copies, waits for them, and re-layouts  78.2 us (32%)
  matrix products  22.8 us (9%)
  other arithmetic  17.4 us (7%)
  between operations  14.4 us (6%)
  starting transfers between devices  6.51 us (3%)
    psum x1, waiting for transfers between devices, body(): predicted = lax.psum(partial_value, 'bank')  58.8 us
    psum x1, waiting for transfers between devices, body(): summed_rows, summed_cols = lax.psum((row_total, col_total), 'cap')  46.9 us
    reshape x4, local copies, waits for them, and re-layouts, diagonals(): flattened[..., :lead_len]  18.5 us
    reshape x4, local copies, waits for them, and re-layouts, diagonals(): flattened = matrix.reshape(matrix.shape[:-2] + (line_count * span_len,))  16.1 us
    reshape x4, local copies, waits for them, and re-layouts, banded(): repeated[..., :band_width * span_len]  13.7 us
    another operation x8, local copies, waits for them, and re-layouts, banded(): repeated = jnp.tile(padded, (1,) * (kernel.ndim - 1) + (band_width,))  12.5 us
    dot_general x2, matrix products, body(): jnp.einsum('cqrkx,cqkj->qrxj', backward, windows[tile_index], preferred_e...  12.5 us
    slice x4, local copies, waits for them, and re-layouts, diagonals(): flattened[..., :lead_len]  8.63 us
  transfers between devices with their start and end apart: 4, of which 2 were waited for; matrix products, arithmetic and copies ran while one was open for 13% of the time, Pallas kernels for 0%

commit v1 on v0

v1 whole, which is shorter than its diff:
```python
import functools

import jax
import jax.numpy as jnp
from jax import lax
from jax.experimental import pallas as pl
from jax.experimental.pallas import tpu as pltpu
from jax.sharding import PartitionSpec as P

TILE = 16
PW = 128
BF = jnp.bfloat16
F32 = jnp.float32
MESH = pl.DeviceIdType.MESH

SPAN = ((0, 128), (0, 256), (0, 256), (0, 256), (0, 256), (128, 128))


def nt(a, b):
    return lax.dot_general(a, b, (((1,), (1,)), ((), ())), preferred_element_type=F32)


def nn(a, b):
    return jnp.dot(a, b, preferred_element_type=F32)


def flip(rows, block):
    i = lax.broadcasted_iota(jnp.int32, (rows, rows), 0)
    j = lax.broadcasted_iota(jnp.int32, (rows, rows), 1)
    same = (i // block) == (j // block)
    return (same & ((i % block) + (j % block) == block - 1)).astype(F32).astype(BF)


def kernel(
    fields, banks, caps, across,
    tile_ref, sat_ref, meas_ref, rowk_ref, colk_ref, pat_hbm,
    out_row, out_col,
    pat, k3, kf, tb, cb, cp, s1, f1, s2, f2, rs, rb, ct, gc, gp, gn, ga,
    pat_sem, k_s, k_r, f1_s, f1_r, f2_s, f2_r, r_s, r_r, g_s, g_r, c_s, c_r,
):
    colours, ranks = 3, 4
    rows_ext = pat.shape[1]
    span = rows_ext - TILE
    me_f = lax.axis_index("field")
    me_b = lax.axis_index("bank")
    me_c = lax.axis_index("cap")
    side_f = (lax.rem(me_f + fields - 1, fields), me_f, lax.rem(me_f + 1, fields))
    bank_at = [lax.rem(me_b + k, banks) for k in range(banks)]
    cap_at = [lax.rem(me_c + k, caps) for k in range(caps)]

    load = pltpu.make_async_copy(pat_hbm.at[0], pat, pat_sem)
    load.start()

    barrier = pltpu.get_barrier_semaphore()
    peers = 0
    for s in range(3):
        for k in range(banks):
            if s != 1 or k != 0:
                pl.semaphore_signal(
                    barrier, inc=1, device_id={"field": side_f[s], "bank": bank_at[k]}, device_id_type=MESH
                )
                peers += 1
    for k in range(1, caps):
        pl.semaphore_signal(barrier, inc=1, device_id={"cap": cap_at[k]}, device_id_type=MESH)
        peers += 1

    uses_one = [tile_ref[t] == 1 for t in range(2)]
    k3[1] = jnp.zeros((48, 512), BF)
    for kind, ref in ((0, rowk_ref), (1, colk_ref)):
        for t in range(2):
            for q in range(colours):
                at = ((kind * 2 + t) * colours + q) * ranks
                first = ref[0, q].astype(F32)
                second = ref[1, q].astype(F32)
                k3[1, at : at + ranks, 0:511] = jnp.where(uses_one[t], second, first).astype(BF)

    pl.semaphore_wait(barrier, peers)
    k_copies = []
    for i, s in enumerate((0, 2)):
        copy = pltpu.make_async_remote_copy(
            src_ref=k3.at[1], dst_ref=k3.at[2 - s], send_sem=k_s.at[i], recv_sem=k_r.at[1 - i],
            device_id={"field": side_f[s]}, device_id_type=MESH,
        )
        copy.start()
        k_copies.append(copy)

    gp[...] = jnp.zeros(gp.shape, F32)
    rb[...] = jnp.zeros(rb.shape, BF)
    ct[...] = jnp.zeros(ct.shape, F32)

    row_half = me_b // 2
    patch_half = lax.rem(me_b, 2)
    first_tile = row_half * across + me_f * (2 * PW // TILE) + patch_half * (PW // TILE)
    sub = lax.broadcasted_iota(jnp.int32, (8, sat_ref.shape[1]), 0)
    hit = (jnp.broadcast_to(sat_ref[0:1, :], (8, sat_ref.shape[1])) == sub + first_tile).astype(F32)
    hit = jnp.max(hit, axis=1, keepdims=True)
    lane_tile = lax.broadcasted_iota(jnp.int32, (8, PW), 1) // TILE
    mine = (lane_tile == lax.broadcasted_iota(jnp.int32, (8, PW), 0)).astype(F32)
    keep = 1.0 - jnp.sum(hit * mine, axis=0, keepdims=True)

    def bands(s):
        taps = k3[s].astype(F32)
        if s == 0:
            taps = taps * (me_f > 0).astype(F32)
        if s == 2:
            taps = taps * (me_f < fields - 1).astype(F32)
        kf[s] = jnp.zeros((48, 1024), F32)
        kf[s, 0:24, 256:768] = pltpu.roll(taps[0:24], 1, 1)
        kf[s, 24:48, 0:512] = taps[24:48]
        for t in range(2):
            p = 2 * s + t
            j0, jw = SPAN[p]
            for q in range(colours):
                for r in range(ranks):
                    at = (t * colours + q) * ranks + r
                    off = 256 + 128 * (3 - p)
                    line = jnp.broadcast_to(kf[s, at : at + 1, off + j0 : off + j0 + 128 + jw], (PW, 128 + jw))
                    tilted = pltpu.roll(line, 0, 1, stride=1, stride_axis=0)
                    tb[q, p, :, r * jw : (r + 1) * jw] = tilted[:, 128:].astype(BF)
                    line = jnp.broadcast_to(kf[s, 24 + at : 25 + at, 0:640], (TILE, 640))
                    tilted = pltpu.roll(line, 0, 1, stride=1, stride_axis=0)
                    at = (p * ranks + r) * TILE
                    cb[q, at : at + TILE, :] = tilted.astype(BF)

    bands(1)
    for i, s in enumerate((0, 2)):
        pltpu.make_async_remote_copy(
            src_ref=k3.at[1], dst_ref=k3.at[s], send_sem=k_s.at[i], recv_sem=k_r.at[i],
            device_id={"field": side_f[s]}, device_id_type=MESH,
        ).wait_recv()
        bands(s)
    load.wait()

    sends = list(k_copies)

    def forward(q):
        for u in range(2):
            passed = nn(cb[q, :, 0:span], pat[q, u * TILE : u * TILE + span, :]).astype(BF)
            for p in range(6):
                j0, jw = SPAN[p]
                for r in range(ranks):
                    at = (p * ranks + r) * TILE
                    cp[q, p, u * TILE : (u + 1) * TILE, r * jw : (r + 1) * jw] = passed[at : at + TILE, j0 : j0 + jw]
        for s in (0, 2, 1):
            for t in range(2):
                p = 2 * s + t
                wide = ranks * SPAN[p][1]
                part = nt(cp[q, p, :, 0:wide], tb[q, p, :, 0:wide])
                for h in range(2):
                    s1[q, s, h * 2 + t] = part[h * TILE : (h + 1) * TILE]
            if s != 1:
                i = s // 2
                copy = pltpu.make_async_remote_copy(
                    src_ref=s1.at[q, s], dst_ref=f1.at[q, 1 - i], send_sem=f1_s.at[q, i], recv_sem=f1_r.at[q, 1 - i],
                    device_id={"field": side_f[s]}, device_id_type=MESH,
                )
                copy.start()
                sends.append(copy)

    def mid_one(q):
        for i in range(2):
            pltpu.make_async_remote_copy(
                src_ref=s1.at[q, 1], dst_ref=f1.at[q, i], send_sem=f1_s.at[q, i], recv_sem=f1_r.at[q, i],
                device_id={"field": side_f[2 * i]}, device_id_type=MESH,
            ).wait_recv()
        s2[q] = s1[q, 1] + f1[q, 0] + f1[q, 1]
        for k in range(1, banks):
            copy = pltpu.make_async_remote_copy(
                src_ref=s2.at[q, bank_at[k]], dst_ref=f2.at[q, banks - k],
                send_sem=f2_s.at[q, k], recv_sem=f2_r.at[q, banks - k],
                device_id={"bank": bank_at[k]}, device_id_type=MESH,
            )
            copy.start()
            sends.append(copy)

    def mid_two(q):
        total = s2[q, me_b]
        for k in range(1, banks):
            pltpu.make_async_remote_copy(
                src_ref=s2.at[q, 0], dst_ref=f2.at[q, k], send_sem=f2_s.at[q, k], recv_sem=f2_r.at[q, k],
                device_id={"bank": bank_at[k]}, device_id_type=MESH,
            ).wait_recv()
            total = total + f2[q, k]
        seen = meas_ref[0, q, pl.ds(row_half * TILE, TILE), pl.ds(patch_half * PW, PW)].astype(F32)
        rs[q, 1, me_b] = (keep * (total - seen)).astype(BF)
        for s in range(3):
            for k in range(banks):
                if s == 1 and k == 0:
                    continue
                copy = pltpu.make_async_remote_copy(
                    src_ref=rs.at[q, 1, me_b], dst_ref=rs.at[q, 2 - s, me_b],
                    send_sem=r_s.at[q, s, k], recv_sem=r_r.at[q, 2 - s, (banks - k) % banks],
                    device_id={"field": side_f[s], "bank": bank_at[k]}, device_id_type=MESH,
                )
                copy.start()
                sends.append(copy)

    def backward(q):
        for s in range(3):
            for k in range(banks):
                if s == 1 and k == 0:
                    continue
                pltpu.make_async_remote_copy(
                    src_ref=rs.at[q, 1, me_b], dst_ref=rs.at[q, s, bank_at[k]],
                    send_sem=r_s.at[q, s, k], recv_sem=r_r.at[q, s, k],
                    device_id={"field": side_f[s], "bank": bank_at[k]}, device_id_type=MESH,
                ).wait_recv()
        for p in range(6):
            s, t = p // 2, p % 2
            j0, jw = SPAN[p]
            wide = ranks * jw
            res = jnp.concatenate([rs[q, s, t], rs[q, s, 2 + t]], axis=0)
            turned = nn(flip(2 * TILE, TILE), res).astype(BF)
            across_x = nt(flip(PW, PW), res).astype(BF)
            back = nn(turned, tb[q, p, :, 0:wide]).astype(BF)
            for u in range(2):
                for r in range(ranks):
                    at = (p * ranks + r) * TILE
                    rb[u, at : at + TILE, j0 : j0 + jw] = back[u * TILE : (u + 1) * TILE, r * jw : (r + 1) * jw]
            for r in range(ranks):
                terms = nn(across_x, cp[q, p, :, r * jw : (r + 1) * jw])
                terms = jnp.concatenate([terms, jnp.zeros((PW, 128), F32)], axis=1)
                tilted = pltpu.roll(terms, 0, 1, stride=1, stride_axis=0)
                line = jnp.sum(tilted, axis=0, keepdims=True)
                low = 128 * (3 - p) + j0
                skip = max(0, -low)
                stop = min(128 + jw, 512 - low)
                at = t * ranks + r
                gp[q, s, at : at + 1, low + skip : low + stop] = line[:, skip:stop]
        ct[:, 0:span] = nt(rb[0], pat[q, 0:span, :]) + nt(rb[1], pat[q, TILE : TILE + span, :])
        for p in range(6):
            for r in range(ranks):
                at = p * ranks + r
                tilted = pltpu.roll(ct[at * TILE : (at + 1) * TILE, :], 0, 1, stride=1, stride_axis=0)
                gc[at : at + 1, :] = jnp.sum(tilted, axis=0, keepdims=True)
        lines = pltpu.roll(gc[...], 640 - (TILE - 1), 1)[:, 0:512]
        for s in range(3):
            gp[q, s, 8:16, :] = lines[8 * s : 8 * s + 8]
        for i, s in enumerate((0, 2)):
            copy = pltpu.make_async_remote_copy(
                src_ref=gp.at[q, s], dst_ref=gn.at[q, 1 - i], send_sem=g_s.at[q, i], recv_sem=g_r.at[q, 1 - i],
                device_id={"field": side_f[s]}, device_id_type=MESH,
            )
            copy.start()
            sends.append(copy)

    one = [jnp.where(u, 1.0, 0.0) for u in uses_one]

    def tail_one(q):
        for i in range(2):
            pltpu.make_async_remote_copy(
                src_ref=gp.at[q, 1], dst_ref=gn.at[q, i], send_sem=g_s.at[q, i], recv_sem=g_r.at[q, i],
                device_id={"field": side_f[2 * i]}, device_id_type=MESH,
            ).wait_recv()
        total = gp[q, 1] + gn[q, 0] + gn[q, 1]
        for kind in range(2):
            a = total[8 * kind : 8 * kind + 4]
            b = total[8 * kind + 4 : 8 * kind + 8]
            ga[q, me_c, 8 * kind : 8 * kind + 4] = a * (1.0 - one[0]) + b * (1.0 - one[1])
            ga[q, me_c, 8 * kind + 4 : 8 * kind + 8] = a * one[0] + b * one[1]
        for k in range(1, caps):
            copy = pltpu.make_async_remote_copy(
                src_ref=ga.at[q, me_c], dst_ref=ga.at[q, me_c], send_sem=c_s.at[q, k], recv_sem=c_r.at[q, caps - k],
                device_id={"cap": cap_at[k]}, device_id_type=MESH,
            )
            copy.start()
            sends.append(copy)

    def tail_two(q):
        for k in range(1, caps):
            pltpu.make_async_remote_copy(
                src_ref=ga.at[q, me_c], dst_ref=ga.at[q, cap_at[k]], send_sem=c_s.at[q, k], recv_sem=c_r.at[q, k],
                device_id={"cap": cap_at[k]}, device_id_type=MESH,
            ).wait_recv()
        total = ga[q, 0]
        for c in range(1, caps):
            total = total + ga[q, c]
        total = total * (1.0 / 32)
        for k in range(2):
            out_row[k, q] = total[4 * k : 4 * k + 4, 0:511]
            out_col[k, q] = total[8 + 4 * k : 12 + 4 * k, 0:511]

    forward(0)
    forward(1)
    mid_one(0)
    forward(2)
    mid_two(0)
    mid_one(1)
    mid_two(1)
    mid_one(2)
    backward(0)
    mid_two(2)
    backward(1)
    tail_one(0)
    backward(2)
    tail_one(1)
    tail_two(0)
    tail_one(2)
    tail_two(1)
    tail_two(2)
    for copy in sends:
        copy.wait_send()


def body(pattern, measured, row_kernels, col_kernels, tile_patch, sat_tiles):
    fields, banks, caps = (lax.axis_size(a) for a in ("field", "bank", "cap"))
    _, colours, rows_ext, strip = pattern.shape
    across = fields * strip // TILE
    vm = pl.BlockSpec(memory_space=pltpu.VMEM)
    dma = pltpu.SemaphoreType.DMA
    out = jax.ShapeDtypeStruct(row_kernels.shape, F32)
    return pl.pallas_call(
        functools.partial(kernel, fields, banks, caps, across),
        out_shape=(out, out),
        in_specs=[pl.BlockSpec(memory_space=pltpu.SMEM), vm, vm, vm, vm, pl.BlockSpec(memory_space=pl.ANY)],
        out_specs=(vm, vm),
        scratch_shapes=[
            pltpu.VMEM((colours, rows_ext, strip), BF),
            pltpu.VMEM((3, 48, 512), BF),
            pltpu.VMEM((3, 48, 1024), F32),
            pltpu.VMEM((colours, 6, PW, 1024), BF),
            pltpu.VMEM((colours, 384, 640), BF),
            pltpu.VMEM((colours, 6, 32, 1024), BF),
            pltpu.VMEM((colours, 3, 4, TILE, PW), F32),
            pltpu.VMEM((colours, 2, 4, TILE, PW), F32),
            pltpu.VMEM((colours, 4, TILE, PW), F32),
            pltpu.VMEM((colours, 4, TILE, PW), F32),
            pltpu.VMEM((colours, 3, 4, TILE, PW), BF),
            pltpu.VMEM((2, 384, strip), BF),
            pltpu.VMEM((384, 640), F32),
            pltpu.VMEM((24, 640), F32),
            pltpu.VMEM((colours, 3, 16, 512), F32),
            pltpu.VMEM((colours, 2, 16, 512), F32),
            pltpu.VMEM((colours, caps, 16, 512), F32),
            dma, dma((2,)), dma((2,)), dma((colours, 2)), dma((colours, 2)),
            dma((colours, banks)), dma((colours, banks)), dma((colours, 3, banks)), dma((colours, 3, banks)),
            dma((colours, 2)), dma((colours, 2)), dma((colours, caps)), dma((colours, caps)),
        ],
        compiler_params=pltpu.CompilerParams(
            collective_id=0, has_side_effects=True, vmem_limit_bytes=40 << 20
        ),
    )(tile_patch, sat_tiles, measured, row_kernels, col_kernels, pattern)


def solution(mesh):
    return jax.shard_map(
        body,
        mesh=mesh,
        in_specs=(
            P("cap", None, None, "field"),
            P("cap", None, None, "field"),
            P("field", None, "bank", None),
            P("field", None, "bank", None),
            P("field"),
            P("cap", None),
        ),
        out_specs=(P("field", None, "bank", None), P("field", None, "bank", None)),
        check_vma=False,
    )
```

time: 246 us -> 67.6 us (0.27)
  waiting for transfers between devices: 106 us -> 0 us
  local copies, waits for them, and re-layouts: 78.2 us -> 5.99 us
  Pallas kernels: 0 us -> 60.6 us
  matrix products: 22.8 us -> 0 us
  other arithmetic: 17.4 us -> 0 us
  between operations: 14.4 us -> 0.65 us
  starting transfers between devices: 6.51 us -> 0 us
    psum x2 -> x0, waiting for transfers between devices: 106 us -> none  [the longest x1 58.8 us: body(): predicted = lax.psum(partial_value, 'bank')]
    pallas_call x0 -> x1, Pallas kernels: none -> 60.6 us  [body(): pl.pallas_call(functools.partial(kernel, fields, banks, caps, across), ou...]
    reshape x12 -> x0, local copies, waits for them, and re-layouts: 48.2 us -> none  [the longest x4 18.5 us: diagonals(): flattened[..., :lead_len]]
    dot_general x12 -> x0, matrix products: 22.8 us -> none  [the longest x2 12.5 us: body(): jnp.einsum('cqrkx,cqkj->qrxj', backward, windows[tile_index], preferred_e...]
    slice x10 -> x0, local copies, waits for them, and re-layouts: 15.3 us -> none  [the longest x4 8.63 us: diagonals(): flattened[..., :lead_len]]
    another operation x8 -> x0, local copies, waits for them, and re-layouts: 12.5 us -> none  [banded(): repeated = jnp.tile(padded, (1,) * (kernel.ndim - 1) + (band_width,))]
    reduce_sum x4 -> x0, other arithmetic: 7.04 us -> none  [diagonals(): return jnp.sum(shaped[..., :tap_count], axis=-2) + last_line]
    ppermute x2 -> x0, starting transfers between devices: 6.21 us -> none  [the longest x1 4.93 us: with_halo(): lax.ppermute(tail, axis, [(i, (i + 1) % count) for i in range(ends)])]
  transfers between devices with their start and end apart: 4 -> 0, of which waited for: 2 -> 0; matrix products, arithmetic and copies ran while one was open for 13% -> 0% of each run, Pallas kernels for 0% -> 0%
where the time goes in v1:
time: 67.6 us; the launch traced here: 67.3 us
  Pallas kernels  60.6 us (90%)
  local copies, waits for them, and re-layouts  5.99 us (9%)
    pallas_call x1, Pallas kernels, body(): pl.pallas_call(functools.partial(kernel, fields, banks, caps, across), ou...  60.6 us
    unnamed x14, local copies, waits for them, and re-layouts  5.99 us

profile of v1, /device:TPU:1, one launch (start us, length us, event | category | flops | bytes accessed | tf_op | source)
XLA Modules:
  0.0 67.3 jit_solution(1781404874417927900)
XLA Ops:
  0.6 0.0 copy-start
  0.6 1.1 %copy-done = bf16[1,3,542,256]{3,2,1,0:T(8,128)(2,1)S(1)} copy-done((bf16[1,3,542,256]{3,2,1,0:T(8,128)(2,1)S(1)}, bf16[1,3,542,256]{3,2,1,0:T(8,128)(2,1)}, u32[]{:S(2)}) %copy-start) | copy-done | bytes 832536
  1.8 0.0 copy-start.1
  1.8 0.8 %copy-done.1 = bf16[1,3,32,256]{3,2,1,0:T(8,128)(2,1)S(1)} copy-done((bf16[1,3,32,256]{3,2,1,0:T(8,128)(2,1)S(1)}, bf16[1,3,32,256]{3,2,1,0:T(8,128)(2,1)}, u32[]{:S(2)}) %copy-start.1) | copy-done | bytes 49176
  2.6 0.0 copy-start.2
  2.6 0.7 %copy-done.2 = bf16[2,3,4,511]{3,2,1,0:T(4,128)(2,1)S(1)} copy-done((bf16[2,3,4,511]{3,2,1,0:T(4,128)(2,1)S(1)}, bf16[2,3,4,511]{3,2,1,0:T(4,128)(2,1)}, u32[]{:S(2)}) %copy-start.2) | copy-done | bytes 24552
  3.3 0.0 copy-start.3
  3.3 0.7 %copy-done.3 = bf16[2,3,4,511]{3,2,1,0:T(4,128)(2,1)S(1)} copy-done((bf16[2,3,4,511]{3,2,1,0:T(4,128)(2,1)S(1)}, bf16[2,3,4,511]{3,2,1,0:T(4,128)(2,1)}, u32[]{:S(2)}) %copy-start.3) | copy-done | bytes 24552
  4.1 0.0 copy-start.4
  4.1 0.7 %copy-done.4 = s32[1,256]{1,0:T(1,128)S(1)} copy-done((s32[1,256]{1,0:T(1,128)S(1)}, s32[1,256]{1,0:T(1,128)}, u32[]{:S(2)}) %copy-start.4) | copy-done | bytes 1048
  4.7 0.0 copy-start.5
  4.7 0.7 copy-done.5
  5.4 60.6 %shard_map.77 = (f32[2,3,4,511]{3,2,1,0:T(4,128)S(1)}, f32[2,3,4,511]{3,2,1,0:T(4,128)S(1)}) custom-call(s32[2]{0:T(128)S(1)} %copy-done.5, s32[1,256]{1,0:T(1,128)S(1)} %copy-done.4, bf16[1,3,32,256]{3,2,1,0:T(8,128)(2,1)S(1)} %copy-done.1, bf16[2,3,4,511]{3,2,1,0:T(4,128)(2,1)S(1)} %copy-done.2, bf16[2,3,4,511]{3,2,1,0:T(4,128)(2,1)S(1)} %copy-done.3, ...), custom_call_target="tpu_custom_call" | custom-call | tf_op jit(solution)/shard_map/pallas_call | solution.py:312
  66.0 0.6 copy.10
  66.6 0.6 copy.11
Async XLA Ops:
  0.6 1.2 %copy-start = (bf16[1,3,542,256]{3,2,1,0:T(8,128)(2,1)S(1)}, bf16[1,3,542,256]{3,2,1,0:T(8,128)(2,1)}, u32[]{:S(2)}) copy-start(bf16[1,3,542,256]{3,2,1,0:T(8,128)(2,1)} %pat_hbm.1) | copy-start | bytes 2497540
  1.8 0.8 %copy-start.1 = (bf16[1,3,32,256]{3,2,1,0:T(8,128)(2,1)S(1)}, bf16[1,3,32,256]{3,2,1,0:T(8,128)(2,1)}, u32[]{:S(2)}) copy-start(bf16[1,3,32,256]{3,2,1,0:T(8,128)(2,1)} %meas_ref.1) | copy-start | bytes 147460
  2.6 0.7 %copy-start.2 = (bf16[2,3,4,511]{3,2,1,0:T(4,128)(2,1)S(1)}, bf16[2,3,4,511]{3,2,1,0:T(4,128)(2,1)}, u32[]{:S(2)}) copy-start(bf16[2,3,4,511]{3,2,1,0:T(4,128)(2,1)} %rowk_ref.1) | copy-start | bytes 73588
  3.3 0.7 %copy-start.3 = (bf16[2,3,4,511]{3,2,1,0:T(4,128)(2,1)S(1)}, bf16[2,3,4,511]{3,2,1,0:T(4,128)(2,1)}, u32[]{:S(2)}) copy-start(bf16[2,3,4,511]{3,2,1,0:T(4,128)(2,1)} %colk_ref.1) | copy-start | bytes 73588
  4.1 0.7 %copy-start.4 = (s32[1,256]{1,0:T(1,128)S(1)}, s32[1,256]{1,0:T(1,128)}, u32[]{:S(2)}) copy-start(s32[1,256]{1,0:T(1,128)} %sat_ref.1) | copy-start | bytes 3076
  4.7 0.7 copy-start.5

commit v2 on v1

v2 whole, which is shorter than its diff:
```python
import functools

import jax
import jax.numpy as jnp
from jax import lax
from jax.experimental import pallas as pl
from jax.experimental.pallas import tpu as pltpu
from jax.sharding import PartitionSpec as P

TILE = 16
PW = 128
BF = jnp.bfloat16
F32 = jnp.float32
MESH = pl.DeviceIdType.MESH

SPAN = ((0, 128), (0, 256), (0, 256), (0, 256), (0, 256), (128, 128))


def nt(a, b):
    return lax.dot_general(a, b, (((1,), (1,)), ((), ())), preferred_element_type=F32)


def nn(a, b):
    return jnp.dot(a, b, preferred_element_type=F32)


def flip(rows, block):
    i = lax.broadcasted_iota(jnp.int32, (rows, rows), 0)
    j = lax.broadcasted_iota(jnp.int32, (rows, rows), 1)
    same = (i // block) == (j // block)
    return (same & ((i % block) + (j % block) == block - 1)).astype(F32).astype(BF)


def kernel(
    fields, banks, caps, across,
    tile_hbm, sat_hbm, meas_hbm, rowk_hbm, colk_hbm, pat_hbm,
    out_row, out_col,
    tile_ref, sat, meas, rowk, colk, pat,
    k3, kf, tb, cb, cp, own, f1s, f1, f2s, f2, rs, rb, ct, gc, gp, gn, ga,
    in_sem, k_s, k_r, f1_s, f1_r, f2_s, f2_r, r_s, r_r, g_s, g_r, c_s, c_r,
):
    colours, ranks = 3, 4
    rows_ext = pat.shape[1]
    span = rows_ext - TILE
    me_f = lax.axis_index("field")
    me_b = lax.axis_index("bank")
    me_c = lax.axis_index("cap")
    side_f = (lax.rem(me_f + fields - 1, fields), me_f, lax.rem(me_f + 1, fields))
    bank_at = [lax.rem(me_b + k, banks) for k in range(banks)]
    cap_at = [lax.rem(me_c + k, caps) for k in range(caps)]

    barrier = pltpu.get_barrier_semaphore()
    for k in (2, 1, 3):
        pl.semaphore_signal(barrier, inc=1, device_id={"bank": bank_at[k]}, device_id_type=MESH)
    for s in (0, 2):
        pl.semaphore_signal(barrier, inc=1, device_id={"field": side_f[s]}, device_id_type=MESH)
    for k in range(1, caps):
        pl.semaphore_signal(barrier, inc=1, device_id={"cap": cap_at[k]}, device_id_type=MESH)

    loads = [
        pltpu.make_async_copy(src, dst, in_sem.at[i])
        for i, (src, dst) in enumerate(
            ((tile_hbm, tile_ref), (rowk_hbm, rowk), (colk_hbm, colk), (sat_hbm, sat), (pat_hbm.at[0], pat), (meas_hbm.at[0], meas))
        )
    ]
    for load in loads:
        load.start()

    gp[...] = jnp.zeros(gp.shape, F32)
    rb[...] = jnp.zeros(rb.shape, BF)
    ct[...] = jnp.zeros(ct.shape, F32)
    k3[1] = jnp.zeros((48, 512), BF)
    kf[...] = jnp.zeros(kf.shape, F32)

    for load in loads[0:4]:
        load.wait()
    uses_one = [tile_ref[t] == 1 for t in range(2)]
    for kind, ref in ((0, rowk), (1, colk)):
        for t in range(2):
            for q in range(colours):
                at = ((kind * 2 + t) * colours + q) * ranks
                first = ref[0, q].astype(F32)
                second = ref[1, q].astype(F32)
                k3[1, at : at + ranks, 0:511] = jnp.where(uses_one[t], second, first).astype(BF)

    pl.semaphore_wait(barrier, 2 + banks - 1 + caps - 1)
    sends = []
    for i, s in enumerate((0, 2)):
        copy = pltpu.make_async_remote_copy(
            src_ref=k3.at[1], dst_ref=k3.at[2 - s], send_sem=k_s.at[i], recv_sem=k_r.at[1 - i],
            device_id={"field": side_f[s]}, device_id_type=MESH,
        )
        copy.start()
        sends.append(copy)

    tiles = 2 * PW // TILE
    sub = lax.broadcasted_iota(jnp.int32, (tiles, sat.shape[1]), 0)
    listed = jnp.broadcast_to(sat[0:1, :], (tiles, sat.shape[1]))
    lane_tile = lax.broadcasted_iota(jnp.int32, (tiles, 2 * PW), 1) // TILE
    mine = (lane_tile == lax.broadcasted_iota(jnp.int32, (tiles, 2 * PW), 0)).astype(F32)
    keep = []
    for h in range(2):
        hit = (listed == sub + (h * across + me_f * tiles)).astype(F32)
        hit = jnp.max(hit, axis=1, keepdims=True)
        line = 1.0 - jnp.sum(hit * mine, axis=0, keepdims=True)
        keep.append(jnp.broadcast_to(line, (TILE, 2 * PW)))
    keep = jnp.concatenate(keep, axis=0)

    def taps(s):
        lines = k3[s].astype(F32)
        if s == 0:
            lines = lines * (me_f > 0).astype(F32)
        if s == 2:
            lines = lines * (me_f < fields - 1).astype(F32)
        kf[s, 0:24, 256:768] = pltpu.roll(lines[0:24], 1, 1)
        kf[s, 24:48, 0:512] = lines[24:48]

    def bands(q, s):
        for t in range(2):
            p = 2 * s + t
            j0, jw = SPAN[p]
            for r in range(ranks):
                at = (t * colours + q) * ranks + r
                off = 256 + 128 * (3 - p)
                line = jnp.broadcast_to(kf[s, at : at + 1, off + j0 : off + j0 + 128 + jw], (PW, 128 + jw))
                tilted = pltpu.roll(line, 0, 1, stride=1, stride_axis=0)
                tb[q, p, :, r * jw : (r + 1) * jw] = tilted[:, 128:].astype(BF)
                line = jnp.broadcast_to(kf[s, 24 + at : 25 + at, 0:640], (TILE, 640))
                tilted = pltpu.roll(line, 0, 1, stride=1, stride_axis=0)
                at = (p * ranks + r) * TILE
                cb[q, at : at + TILE, :] = tilted.astype(BF)

    def image(q, s):
        at0 = 2 * s * ranks * TILE
        for u in range(2):
            passed = nn(cb[q, at0 : at0 + 128, 0:span], pat[q, u * TILE : u * TILE + span, :]).astype(BF)
            for t in range(2):
                p = 2 * s + t
                j0, jw = SPAN[p]
                for r in range(ranks):
                    at = (t * ranks + r) * TILE
                    cp[q, p, u * TILE : (u + 1) * TILE, r * jw : (r + 1) * jw] = passed[at : at + TILE, j0 : j0 + jw]
        parts = []
        for t in range(2):
            p = 2 * s + t
            wide = ranks * SPAN[p][1]
            parts.append(nt(cp[q, p, :, 0:wide], tb[q, p, :, 0:wide]))
        return jnp.concatenate(parts, axis=1)

    def side_copy(src, dst, i, send, recv):
        return pltpu.make_async_remote_copy(
            src_ref=src, dst_ref=dst(1 - i), send_sem=send(i), recv_sem=recv(1 - i),
            device_id={"field": side_f[2 * i]}, device_id_type=MESH,
        )

    def side_wait(src, dst, i, send, recv):
        pltpu.make_async_remote_copy(
            src_ref=src, dst_ref=dst(i), send_sem=send(i), recv_sem=recv(i),
            device_id={"field": side_f[2 * i]}, device_id_type=MESH,
        ).wait_recv()

    taps(1)
    for q in range(colours):
        bands(q, 1)
    loads[4].wait()
    for q in range(colours):
        own[q] = image(q, 1)
    for i, s in enumerate((0, 2)):
        side_wait(k3.at[1], lambda i: k3.at[2 * i], i, lambda i: k_s.at[i], lambda i: k_r.at[i])
        taps(s)
    loads[5].wait()

    def forward(q):
        for i, s in enumerate((0, 2)):
            bands(q, s)
            f1s[q, i] = image(q, s).astype(BF)
            copy = side_copy(f1s.at[q, i], lambda i: f1.at[q, i], i, lambda i: f1_s.at[q, i], lambda i: f1_r.at[q, i])
            copy.start()
            sends.append(copy)

    def mid_one(q):
        for i in range(2):
            side_wait(f1s.at[q, i], lambda i: f1.at[q, i], i, lambda i: f1_s.at[q, i], lambda i: f1_r.at[q, i])
        total = own[q] + f1[q, 0].astype(F32) + f1[q, 1].astype(F32)
        own[q] = total
        f2s[q] = total.astype(BF)
        for k in (2, 1, 3):
            copy = pltpu.make_async_remote_copy(
                src_ref=f2s.at[q], dst_ref=f2.at[q, banks - k],
                send_sem=f2_s.at[q, k], recv_sem=f2_r.at[q, banks - k],
                device_id={"bank": bank_at[k]}, device_id_type=MESH,
            )
            copy.start()
            sends.append(copy)

    def mid_two(q):
        total = own[q] - meas[q].astype(F32)
        for k in range(1, banks):
            pltpu.make_async_remote_copy(
                src_ref=f2s.at[q], dst_ref=f2.at[q, k], send_sem=f2_s.at[q, k], recv_sem=f2_r.at[q, k],
                device_id={"bank": bank_at[k]}, device_id_type=MESH,
            ).wait_recv()
            total = total + f2[q, k].astype(F32)
        rs[q, 1] = (keep * total).astype(BF)
        for i in range(2):
            copy = side_copy(rs.at[q, 1], lambda i: rs.at[q, 2 * i], i, lambda i: r_s.at[q, i], lambda i: r_r.at[q, i])
            copy.start()
            sends.append(copy)

    def residual_wait(q):
        for i in range(2):
            side_wait(rs.at[q, 1], lambda i: rs.at[q, 2 * i], i, lambda i: r_s.at[q, i], lambda i: r_r.at[q, i])

    turn_rows = flip(2 * TILE, TILE)
    turn_cols = flip(PW, PW)

    def backward(q, s):
        for t in range(2):
            p = 2 * s + t
            j0, jw = SPAN[p]
            wide = ranks * jw
            res = rs[q, s, :, t * PW : (t + 1) * PW]
            turned = nn(turn_rows, res).astype(BF)
            across_x = nt(turn_cols, res).astype(BF)
            back = nn(turned, tb[q, p, :, 0:wide]).astype(BF)
            for u in range(2):
                for r in range(ranks):
                    at = (p * ranks + r) * TILE
                    rb[u, at : at + TILE, j0 : j0 + jw] = back[u * TILE : (u + 1) * TILE, r * jw : (r + 1) * jw]
            for r in range(ranks):
                terms = nn(across_x, cp[q, p, :, r * jw : (r + 1) * jw])
                terms = jnp.concatenate([terms, jnp.zeros((PW, 128), F32)], axis=1)
                tilted = pltpu.roll(terms, 0, 1, stride=1, stride_axis=0)
                line = jnp.sum(tilted, axis=0, keepdims=True)
                low = 128 * (3 - p) + j0
                skip = max(0, -low)
                stop = min(128 + jw, 512 - low)
                at = t * ranks + r
                gp[q, s, at : at + 1, low + skip : low + stop] = line[:, skip:stop]
        at0 = 2 * s * ranks * TILE
        ct[at0 : at0 + 128, 0:span] = nt(rb[0, at0 : at0 + 128], pat[q, 0:span, :]) + nt(
            rb[1, at0 : at0 + 128], pat[q, TILE : TILE + span, :]
        )
        for at in range(2 * s * ranks, 2 * (s + 1) * ranks):
            tilted = pltpu.roll(ct[at * TILE : (at + 1) * TILE, :], 0, 1, stride=1, stride_axis=0)
            gc[at : at + 1, :] = jnp.sum(tilted, axis=0, keepdims=True)
        lines = pltpu.roll(gc[8 * s : 8 * s + 8], 640 - (TILE - 1), 1)
        gp[q, s, 8:16, :] = lines[:, 0:512]

    def backward_sides(q):
        residual_wait(q)
        for i in range(2):
            backward(q, 2 * i)
            copy = side_copy(gp.at[q, 2 * i], lambda i: gn.at[q, i], i, lambda i: g_s.at[q, i], lambda i: g_r.at[q, i])
            copy.start()
            sends.append(copy)

    one = [jnp.where(u, 1.0, 0.0) for u in uses_one]

    def tail_one(q):
        for i in range(2):
            side_wait(gp.at[q, 1], lambda i: gn.at[q, i], i, lambda i: g_s.at[q, i], lambda i: g_r.at[q, i])
        total = gp[q, 1] + gn[q, 0] + gn[q, 1]
        for kind in range(2):
            a = total[8 * kind : 8 * kind + 4]
            b = total[8 * kind + 4 : 8 * kind + 8]
            ga[q, me_c, 8 * kind : 8 * kind + 4] = a * (1.0 - one[0]) + b * (1.0 - one[1])
            ga[q, me_c, 8 * kind + 4 : 8 * kind + 8] = a * one[0] + b * one[1]
        for k in range(1, caps):
            copy = pltpu.make_async_remote_copy(
                src_ref=ga.at[q, me_c], dst_ref=ga.at[q, me_c], send_sem=c_s.at[q, k], recv_sem=c_r.at[q, caps - k],
                device_id={"cap": cap_at[k]}, device_id_type=MESH,
            )
            copy.start()
            sends.append(copy)

    def tail_two(q):
        for k in range(1, caps):
            pltpu.make_async_remote_copy(
                src_ref=ga.at[q, me_c], dst_ref=ga.at[q, cap_at[k]], send_sem=c_s.at[q, k], recv_sem=c_r.at[q, k],
                device_id={"cap": cap_at[k]}, device_id_type=MESH,
            ).wait_recv()
        total = ga[q, 0]
        for c in range(1, caps):
            total = total + ga[q, c]
        total = total * (1.0 / 32)
        for k in range(2):
            out_row[k, q] = total[4 * k : 4 * k + 4, 0:511]
            out_col[k, q] = total[8 + 4 * k : 12 + 4 * k, 0:511]

    forward(0)
    forward(1)
    forward(2)
    mid_one(0)
    mid_one(1)
    mid_one(2)
    mid_two(0)
    backward(0, 1)
    mid_two(1)
    backward(1, 1)
    mid_two(2)
    backward(2, 1)
    backward_sides(0)
    backward_sides(1)
    backward_sides(2)
    tail_one(0)
    tail_one(1)
    tail_one(2)
    tail_two(0)
    tail_two(1)
    tail_two(2)
    for copy in sends:
        copy.wait_send()


def body(pattern, measured, row_kernels, col_kernels, tile_patch, sat_tiles):
    fields, banks, caps = (lax.axis_size(a) for a in ("field", "bank", "cap"))
    _, colours, rows_ext, strip = pattern.shape
    across = fields * strip // TILE
    vm = pl.BlockSpec(memory_space=pltpu.VMEM)
    hbm = pl.BlockSpec(memory_space=pltpu.HBM)
    dma = pltpu.SemaphoreType.DMA
    out = jax.ShapeDtypeStruct(row_kernels.shape, F32)
    return pl.pallas_call(
        functools.partial(kernel, fields, banks, caps, across),
        out_shape=(out, out),
        in_specs=[hbm] * 6,
        out_specs=(vm, vm),
        scratch_shapes=[
            pltpu.SMEM(tile_patch.shape, jnp.int32),
            pltpu.VMEM(sat_tiles.shape, jnp.int32),
            pltpu.VMEM(measured.shape[1:], BF),
            pltpu.VMEM(row_kernels.shape, BF),
            pltpu.VMEM(col_kernels.shape, BF),
            pltpu.VMEM((colours, rows_ext, strip), BF),
            pltpu.VMEM((3, 48, 512), BF),
            pltpu.VMEM((3, 48, 1024), F32),
            pltpu.VMEM((colours, 6, PW, 1024), BF),
            pltpu.VMEM((colours, 384, 640), BF),
            pltpu.VMEM((colours, 6, 32, 1024), BF),
            pltpu.VMEM((colours, 32, strip), F32),
            pltpu.VMEM((colours, 2, 32, strip), BF),
            pltpu.VMEM((colours, 2, 32, strip), BF),
            pltpu.VMEM((colours, 32, strip), BF),
            pltpu.VMEM((colours, 4, 32, strip), BF),
            pltpu.VMEM((colours, 3, 32, strip), BF),
            pltpu.VMEM((2, 384, strip), BF),
            pltpu.VMEM((384, 640), F32),
            pltpu.VMEM((24, 640), F32),
            pltpu.VMEM((colours, 3, 16, 512), F32),
            pltpu.VMEM((colours, 2, 16, 512), F32),
            pltpu.VMEM((colours, caps, 16, 512), F32),
            dma((6,)), dma((2,)), dma((2,)), dma((colours, 2)), dma((colours, 2)),
            dma((colours, banks)), dma((colours, banks)), dma((colours, 2)), dma((colours, 2)),
            dma((colours, 2)), dma((colours, 2)), dma((colours, caps)), dma((colours, caps)),
        ],
        compiler_params=pltpu.CompilerParams(
            collective_id=0, has_side_effects=True, vmem_limit_bytes=62 << 20
        ),
    )(tile_patch, sat_tiles, measured, row_kernels, col_kernels, pattern)


def solution(mesh):
    return jax.shard_map(
        body,
        mesh=mesh,
        in_specs=(
            P("cap", None, None, "field"),
            P("cap", None, None, "field"),
            P("field", None, "bank", None),
            P("field", None, "bank", None),
            P("field"),
            P("cap", None),
        ),
        out_specs=(P("field", None, "bank", None), P("field", None, "bank", None)),
        check_vma=False,
    )
```

time: 67.6 us -> 51.5 us (0.76)
  Pallas kernels: 60.6 us -> 48.6 us
  local copies, waits for them, and re-layouts: 5.99 us -> 2.06 us
    pallas_call x1, Pallas kernels: 60.6 us -> 48.6 us  [body(): pl.pallas_call(functools.partial(kernel, fields, banks, caps, across), ou...]
    unnamed x14 -> x4, local copies, waits for them, and re-layouts: 5.99 us -> 2.06 us
where the time goes in v2:
time: 51.5 us; the launch traced here: 51.3 us
  Pallas kernels  48.6 us (94%)
  local copies, waits for them, and re-layouts  2.06 us (4%)
  between operations  0.65 us (1%)
    pallas_call x1, Pallas kernels, body(): pl.pallas_call(functools.partial(kernel, fields, banks, caps, across), ou...  48.6 us
    unnamed x4, local copies, waits for them, and re-layouts  2.06 us

profile of v2, /device:TPU:1, one launch (start us, length us, event | category | flops | bytes accessed | tf_op | source)
XLA Modules:
  0.0 51.3 jit_solution(77815476657172951)
XLA Ops:
  0.6 48.6 %shard_map.77 = (f32[2,3,4,511]{3,2,1,0:T(4,128)}, f32[2,3,4,511]{3,2,1,0:T(4,128)}) custom-call(s32[2]{0:T(128)} %tile_hbm.1, s32[1,256]{1,0:T(1,128)} %sat_hbm.1, bf16[1,3,32,256]{3,2,1,0:T(8,128)(2,1)} %meas_hbm.1, bf16[2,3,4,511]{3,2,1,0:T(4,128)(2,1)} %rowk_hbm.1, bf16[2,3,4,511]{3,2,1,0:T(4,128)(2,1)} %colk_hbm.1, bf16[1,3,542,256]{3,2,1,0:T(8,128)(2,1)} %pat_hbm.1), custom_call_target="tpu_custom_call" | custom-call | tf_op jit(solution)/shard_map/pallas_call | solution.py:324
  49.3 0.0 copy-start
  49.3 1.4 %copy.10 = f32[2,3,4,511]{3,2,1,0:T(4,128)} copy(f32[2,3,4,511]{3,2,1,0:T(4,128)} %get-tuple-element.4) | data formatting | bytes 98112
  50.7 0.0 copy-done
  50.7 0.6 %copy.11 = f32[2,3,4,511]{3,2,1,0:T(4,128)} copy(f32[2,3,4,511]{3,2,1,0:T(4,128)S(1)} %copy-done) | data formatting | bytes 98112
Async XLA Ops:
  49.3 1.4 %copy-start = (f32[2,3,4,511]{3,2,1,0:T(4,128)S(1)}, f32[2,3,4,511]{3,2,1,0:T(4,128)}, u32[]{:S(2)}) copy-start(f32[2,3,4,511]{3,2,1,0:T(4,128)} %get-tuple-element.5) | copy-start | bytes 147172

commit v3 on v2

--- a/solution.py
+++ b/solution.py
@@ -14,6 +14,8 @@
 MESH = pl.DeviceIdType.MESH
 
 SPAN = ((0, 128), (0, 256), (0, 256), (0, 256), (0, 256), (128, 128))
+FIRST = (0, 256, 128)
+PACK = {0: (0, 128), 1: (128, 256), 4: (0, 256), 5: (256, 128)}
 
 
 def nt(a, b):
@@ -36,8 +38,8 @@
     tile_hbm, sat_hbm, meas_hbm, rowk_hbm, colk_hbm, pat_hbm,
     out_row, out_col,
     tile_ref, sat, meas, rowk, colk, pat,
-    k3, kf, tb, cb, cp, own, f1s, f1, f2s, f2, rs, rb, ct, gc, gp, gn, ga,
-    in_sem, k_s, k_r, f1_s, f1_r, f2_s, f2_r, r_s, r_r, g_s, g_r, c_s, c_r,
+    k3, kf, tb, cb, cp, own, f1s, f1, f2s, f2, rs, rb, ct, gc, gp, gq, gs, gn, ga,
+    in_sem, k_s, k_r, f1_s, f1_r, f2_s, f2_r, r_s, r_r, g_s, g_r, c_s, c_r, seen,
 ):
     colours, ranks = 3, 4
     rows_ext = pat.shape[1]
@@ -50,7 +52,7 @@
     cap_at = [lax.rem(me_c + k, caps) for k in range(caps)]
 
     barrier = pltpu.get_barrier_semaphore()
-    for k in (2, 1, 3):
+    for k in (1, banks - 1):
         pl.semaphore_signal(barrier, inc=1, device_id={"bank": bank_at[k]}, device_id_type=MESH)
     for s in (0, 2):
         pl.semaphore_signal(barrier, inc=1, device_id={"field": side_f[s]}, device_id_type=MESH)
@@ -66,7 +68,6 @@
     for load in loads:
         load.start()
 
-    gp[...] = jnp.zeros(gp.shape, F32)
     rb[...] = jnp.zeros(rb.shape, BF)
     ct[...] = jnp.zeros(ct.shape, F32)
     k3[1] = jnp.zeros((48, 512), BF)
@@ -83,7 +84,7 @@
                 second = ref[1, q].astype(F32)
                 k3[1, at : at + ranks, 0:511] = jnp.where(uses_one[t], second, first).astype(BF)
 
-    pl.semaphore_wait(barrier, 2 + banks - 1 + caps - 1)
+    pl.semaphore_wait(barrier, 2 + 2 + caps - 1)
     sends = []
     for i, s in enumerate((0, 2)):
         copy = pltpu.make_async_remote_copy(
@@ -92,6 +93,7 @@
         )
         copy.start()
         sends.append(copy)
+    pl.semaphore_signal(seen, inc=1, device_id={"bank": bank_at[banks - 1]}, device_id_type=MESH)
 
     tiles = 2 * PW // TILE
     sub = lax.broadcasted_iota(jnp.int32, (tiles, sat.shape[1]), 0)
@@ -127,19 +129,23 @@
                 tb[q, p, :, r * jw : (r + 1) * jw] = tilted[:, 128:].astype(BF)
                 line = jnp.broadcast_to(kf[s, 24 + at : 25 + at, 0:640], (TILE, 640))
                 tilted = pltpu.roll(line, 0, 1, stride=1, stride_axis=0)
-                at = (p * ranks + r) * TILE
+                at = FIRST[s] + (t * ranks + r) * TILE
                 cb[q, at : at + TILE, :] = tilted.astype(BF)
 
+    def columns(q, strips):
+        at0 = FIRST[strips[0]]
+        count = len(strips) * 2 * ranks * TILE
+        for u in range(2):
+            passed = nn(cb[q, at0 : at0 + count, 0:span], pat[q, u * TILE : u * TILE + span, :]).astype(BF)
+            for s in strips:
+                for t in range(2):
+                    p = 2 * s + t
+                    j0, jw = SPAN[p]
+                    for r in range(ranks):
+                        at = FIRST[s] - at0 + (t * ranks + r) * TILE
+                        cp[q, p, u * TILE : (u + 1) * TILE, r * jw : (r + 1) * jw] = passed[at : at + TILE, j0 : j0 + jw]
+
     def image(q, s):
-        at0 = 2 * s * ranks * TILE
-        for u in range(2):
-            passed = nn(cb[q, at0 : at0 + 128, 0:span], pat[q, u * TILE : u * TILE + span, :]).astype(BF)
-            for t in range(2):
-                p = 2 * s + t
-                j0, jw = SPAN[p]
-                for r in range(ranks):
-                    at = (t * ranks + r) * TILE
-                    cp[q, p, u * TILE : (u + 1) * TILE, r * jw : (r + 1) * jw] = passed[at : at + TILE, j0 : j0 + jw]
         parts = []
         for t in range(2):
             p = 2 * s + t
@@ -164,15 +170,19 @@
         bands(q, 1)
     loads[4].wait()
     for q in range(colours):
+        columns(q, (1,))
         own[q] = image(q, 1)
     for i, s in enumerate((0, 2)):
         side_wait(k3.at[1], lambda i: k3.at[2 * i], i, lambda i: k_s.at[i], lambda i: k_r.at[i])
         taps(s)
     loads[5].wait()
+    pl.semaphore_wait(seen, 1)
 
     def forward(q):
+        for s in (0, 2):
+            bands(q, s)
+        columns(q, (0, 2))
         for i, s in enumerate((0, 2)):
-            bands(q, s)
             f1s[q, i] = image(q, s).astype(BF)
             copy = side_copy(f1s.at[q, i], lambda i: f1.at[q, i], i, lambda i: f1_s.at[q, i], lambda i: f1_r.at[q, i])
             copy.start()
@@ -214,58 +224,64 @@
     turn_rows = flip(2 * TILE, TILE)
     turn_cols = flip(PW, PW)
 
-    def backward(q, s):
-        for t in range(2):
-            p = 2 * s + t
-            j0, jw = SPAN[p]
-            wide = ranks * jw
-            res = rs[q, s, :, t * PW : (t + 1) * PW]
-            turned = nn(turn_rows, res).astype(BF)
-            across_x = nt(turn_cols, res).astype(BF)
-            back = nn(turned, tb[q, p, :, 0:wide]).astype(BF)
-            for u in range(2):
+    def backward(q, strips):
+        for s in strips:
+            turned = nn(turn_rows, rs[q, s]).astype(BF)
+            for t in range(2):
+                p = 2 * s + t
+                j0, jw = SPAN[p]
+                wide = ranks * jw
+                across_x = nt(turn_cols, rs[q, s, :, t * PW : (t + 1) * PW]).astype(BF)
+                back = nn(turned[:, t * PW : (t + 1) * PW], tb[q, p, :, 0:wide]).astype(BF)
+                for u in range(2):
+                    for r in range(ranks):
+                        at = FIRST[s] + (t * ranks + r) * TILE
+                        rb[u, at : at + TILE, j0 : j0 + jw] = back[u * TILE : (u + 1) * TILE, r * jw : (r + 1) * jw]
                 for r in range(ranks):
-                    at = (p * ranks + r) * TILE
-                    rb[u, at : at + TILE, j0 : j0 + jw] = back[u * TILE : (u + 1) * TILE, r * jw : (r + 1) * jw]
-            for r in range(ranks):
-                terms = nn(across_x, cp[q, p, :, r * jw : (r + 1) * jw])
-                terms = jnp.concatenate([terms, jnp.zeros((PW, 128), F32)], axis=1)
-                tilted = pltpu.roll(terms, 0, 1, stride=1, stride_axis=0)
-                line = jnp.sum(tilted, axis=0, keepdims=True)
-                low = 128 * (3 - p) + j0
-                skip = max(0, -low)
-                stop = min(128 + jw, 512 - low)
-                at = t * ranks + r
-                gp[q, s, at : at + 1, low + skip : low + stop] = line[:, skip:stop]
-        at0 = 2 * s * ranks * TILE
-        ct[at0 : at0 + 128, 0:span] = nt(rb[0, at0 : at0 + 128], pat[q, 0:span, :]) + nt(
-            rb[1, at0 : at0 + 128], pat[q, TILE : TILE + span, :]
-        )
-        for at in range(2 * s * ranks, 2 * (s + 1) * ranks):
+                    terms = nn(across_x, cp[q, p, :, r * jw : (r + 1) * jw])
+                    terms = jnp.concatenate([terms, jnp.zeros((PW, 128), F32)], axis=1)
+                    tilted = pltpu.roll(terms, 0, 1, stride=1, stride_axis=0)
+                    line = jnp.sum(tilted, axis=0, keepdims=True)
+                    low = 128 * (3 - p) + j0
+                    skip = max(0, -low)
+                    stop = min(128 + jw, 512 - low)
+                    at = t * ranks + r
+                    if s == 1:
+                        both = [line[:, 0:384], jnp.zeros((1, 128), F32)]
+                        gp[at : at + 1, :] = jnp.concatenate(both if t else both[::-1], axis=1)
+                    else:
+                        off, wide_off = PACK[p]
+                        gq[s // 2, r : r + 1, off : off + wide_off] = line[:, skip:stop]
+        at0 = FIRST[strips[0]]
+        at1 = at0 + len(strips) * 2 * ranks * TILE
+        ct[at0:at1, 0:span] = nt(rb[0, at0:at1], pat[q, 0:span, :]) + nt(rb[1, at0:at1], pat[q, TILE : TILE + span, :])
+        for at in range(at0 // TILE, at1 // TILE):
             tilted = pltpu.roll(ct[at * TILE : (at + 1) * TILE, :], 0, 1, stride=1, stride_axis=0)
             gc[at : at + 1, :] = jnp.sum(tilted, axis=0, keepdims=True)
-        lines = pltpu.roll(gc[8 * s : 8 * s + 8], 640 - (TILE - 1), 1)
-        gp[q, s, 8:16, :] = lines[:, 0:512]
-
-    def backward_sides(q):
-        residual_wait(q)
-        for i in range(2):
-            backward(q, 2 * i)
-            copy = side_copy(gp.at[q, 2 * i], lambda i: gn.at[q, i], i, lambda i: g_s.at[q, i], lambda i: g_r.at[q, i])
-            copy.start()
-            sends.append(copy)
-
-    one = [jnp.where(u, 1.0, 0.0) for u in uses_one]
-
-    def tail_one(q):
-        for i in range(2):
-            side_wait(gp.at[q, 1], lambda i: gn.at[q, i], i, lambda i: g_s.at[q, i], lambda i: g_r.at[q, i])
-        total = gp[q, 1] + gn[q, 0] + gn[q, 1]
-        for kind in range(2):
-            a = total[8 * kind : 8 * kind + 4]
-            b = total[8 * kind + 4 : 8 * kind + 8]
-            ga[q, me_c, 8 * kind : 8 * kind + 4] = a * (1.0 - one[0]) + b * (1.0 - one[1])
-            ga[q, me_c, 8 * kind + 4 : 8 * kind + 8] = a * one[0] + b * one[1]
+        for s in strips:
+            at = FIRST[s] // TILE
+            lines = pltpu.roll(gc[at : at + 8], 640 - (TILE - 1), 1)
+            if s == 1:
+                gp[8:16, :] = lines[:, 0:512]
+            else:
+                last = [lines[0:4, 384:512], lines[4:8, 384:512], jnp.zeros((4, 128), F32)]
+                low = jnp.concatenate([gq[s // 2], jnp.concatenate(last, axis=1)], axis=0)
+                gs[q, s // 2] = jnp.concatenate([lines[:, 0:384], low], axis=0).astype(BF)
+
+    def unpack(m, i):
+        ends = jnp.concatenate([m[12:16, 0:128], m[12:16, 128:256]], axis=0)
+        cols = jnp.concatenate([m[0:8], ends], axis=1)
+        parts = []
+        for t in range(2):
+            p = 4 * (1 - i) + t
+            off, wide = PACK[p]
+            piece = [m[8:12, off : off + wide], jnp.zeros((4, 512 - wide), F32)]
+            parts.append(jnp.concatenate(piece[::-1] if i == 1 else piece, axis=1))
+        return jnp.concatenate([*parts, cols], axis=0)
+
+    def backward_own(q):
+        backward(q, (1,))
+        ga[q, me_c] = gp[...]
         for k in range(1, caps):
             copy = pltpu.make_async_remote_copy(
                 src_ref=ga.at[q, me_c], dst_ref=ga.at[q, me_c], send_sem=c_s.at[q, k], recv_sem=c_r.at[q, caps - k],
@@ -274,19 +290,47 @@
             copy.start()
             sends.append(copy)
 
-    def tail_two(q):
+    def backward_sides(q):
+        residual_wait(q)
+        backward(q, (0, 2))
+        for i in range(2):
+            for k in range(caps):
+                copy = pltpu.make_async_remote_copy(
+                    src_ref=gs.at[q, i], dst_ref=gn.at[q, 1 - i, me_c],
+                    send_sem=g_s.at[q, i, k], recv_sem=g_r.at[q, 1 - i, (caps - k) % caps],
+                    device_id={"field": side_f[2 * i], "cap": cap_at[k]}, device_id_type=MESH,
+                )
+                copy.start()
+                sends.append(copy)
+
+    one = [jnp.where(u, 1.0, 0.0) for u in uses_one]
+
+    def tail(q):
         for k in range(1, caps):
             pltpu.make_async_remote_copy(
                 src_ref=ga.at[q, me_c], dst_ref=ga.at[q, cap_at[k]], send_sem=c_s.at[q, k], recv_sem=c_r.at[q, k],
                 device_id={"cap": cap_at[k]}, device_id_type=MESH,
             ).wait_recv()
+        for i in range(2):
+            for k in range(caps):
+                pltpu.make_async_remote_copy(
+                    src_ref=gs.at[q, i], dst_ref=gn.at[q, i, cap_at[k]], send_sem=g_s.at[q, i, k], recv_sem=g_r.at[q, i, k],
+                    device_id={"field": side_f[2 * i], "cap": cap_at[k]}, device_id_type=MESH,
+                ).wait_recv()
         total = ga[q, 0]
         for c in range(1, caps):
             total = total + ga[q, c]
+        for i in range(2):
+            side = gn[q, i, 0].astype(F32)
+            for c in range(1, caps):
+                side = side + gn[q, i, c].astype(F32)
+            total = total + unpack(side, i)
         total = total * (1.0 / 32)
-        for k in range(2):
-            out_row[k, q] = total[4 * k : 4 * k + 4, 0:511]
-            out_col[k, q] = total[8 + 4 * k : 12 + 4 * k, 0:511]
+        for kind, out in ((0, out_row), (1, out_col)):
+            a = total[8 * kind : 8 * kind + 4, 0:511]
+            b = total[8 * kind + 4 : 8 * kind + 8, 0:511]
+            out[0, q] = a * (1.0 - one[0]) + b * (1.0 - one[1])
+            out[1, q] = a * one[0] + b * one[1]
 
     forward(0)
     forward(1)
@@ -295,20 +339,17 @@
     mid_one(1)
     mid_one(2)
     mid_two(0)
-    backward(0, 1)
+    backward_own(0)
     mid_two(1)
-    backward(1, 1)
+    backward_own(1)
     mid_two(2)
-    backward(2, 1)
+    backward_own(2)
     backward_sides(0)
     backward_sides(1)
     backward_sides(2)
-    tail_one(0)
-    tail_one(1)
-    tail_one(2)
-    tail_two(0)
-    tail_two(1)
-    tail_two(2)
+    tail(0)
+    tail(1)
+    tail(2)
     for copy in sends:
         copy.wait_send()
 
@@ -347,12 +388,15 @@
             pltpu.VMEM((2, 384, strip), BF),
             pltpu.VMEM((384, 640), F32),
             pltpu.VMEM((24, 640), F32),
-            pltpu.VMEM((colours, 3, 16, 512), F32),
-            pltpu.VMEM((colours, 2, 16, 512), F32),
+            pltpu.VMEM((16, 512), F32),
+            pltpu.VMEM((2, 4, 384), F32),
+            pltpu.VMEM((colours, 2, 16, 384), BF),
+            pltpu.VMEM((colours, 2, caps, 16, 384), BF),
             pltpu.VMEM((colours, caps, 16, 512), F32),
             dma((6,)), dma((2,)), dma((2,)), dma((colours, 2)), dma((colours, 2)),
             dma((colours, banks)), dma((colours, banks)), dma((colours, 2)), dma((colours, 2)),
-            dma((colours, 2)), dma((colours, 2)), dma((colours, caps)), dma((colours, caps)),
+            dma((colours, 2, caps)), dma((colours, 2, caps)), dma((colours, caps)), dma((colours, caps)),
+            pltpu.SemaphoreType.REGULAR,
         ],
         compiler_params=pltpu.CompilerParams(
             collective_id=0, has_side_effects=True, vmem_limit_bytes=62 << 20

time: 51.5 us -> 48 us (0.932)
  Pallas kernels: 48.6 us -> 45.2 us
    pallas_call x1, Pallas kernels: 48.6 us -> 45.2 us  [body(): pl.pallas_call(functools.partial(kernel, fields, banks, caps, across), ou...]
where the time goes in v3:
time: 48 us; the launch traced here: 47.9 us
  Pallas kernels  45.2 us (94%)
  local copies, waits for them, and re-layouts  2.06 us (4%)
  between operations  0.65 us (1%)
    pallas_call x1, Pallas kernels, body(): pl.pallas_call(functools.partial(kernel, fields, banks, caps, across), ou...  45.2 us
    unnamed x4, local copies, waits for them, and re-layouts  2.06 us

profile of v3, /device:TPU:1, one launch (start us, length us, event | category | flops | bytes accessed | tf_op | source)
XLA Modules:
  0.0 47.9 jit_solution(16411303245473182809)
XLA Ops:
  0.6 45.2 %shard_map.77 = (f32[2,3,4,511]{3,2,1,0:T(4,128)}, f32[2,3,4,511]{3,2,1,0:T(4,128)}) custom-call(s32[2]{0:T(128)} %tile_hbm.1, s32[1,256]{1,0:T(1,128)} %sat_hbm.1, bf16[1,3,32,256]{3,2,1,0:T(8,128)(2,1)} %meas_hbm.1, bf16[2,3,4,511]{3,2,1,0:T(4,128)(2,1)} %rowk_hbm.1, bf16[2,3,4,511]{3,2,1,0:T(4,128)(2,1)} %colk_hbm.1, bf16[1,3,542,256]{3,2,1,0:T(8,128)(2,1)} %pat_hbm.1), custom_call_target="tpu_custom_call" | custom-call | tf_op jit(solution)/shard_map/pallas_call | solution.py:365
  45.8 0.0 copy-start
  45.8 1.4 %copy.10 = f32[2,3,4,511]{3,2,1,0:T(4,128)} copy(f32[2,3,4,511]{3,2,1,0:T(4,128)} %get-tuple-element.4) | data formatting | bytes 98112
  47.2 0.0 copy-done
  47.2 0.6 %copy.11 = f32[2,3,4,511]{3,2,1,0:T(4,128)} copy(f32[2,3,4,511]{3,2,1,0:T(4,128)S(1)} %copy-done) | data formatting | bytes 98112
Async XLA Ops:
  45.8 1.4 %copy-start = (f32[2,3,4,511]{3,2,1,0:T(4,128)S(1)}, f32[2,3,4,511]{3,2,1,0:T(4,128)}, u32[]{:S(2)}) copy-start(f32[2,3,4,511]{3,2,1,0:T(4,128)} %get-tuple-element.5) | copy-start | bytes 147172

commit v4 on v3

--- a/solution.py
+++ b/solution.py
@@ -51,11 +51,26 @@
     bank_at = [lax.rem(me_b + k, banks) for k in range(banks)]
     cap_at = [lax.rem(me_c + k, caps) for k in range(caps)]
 
+    has = (me_f > 0, me_f < fields - 1)
+    ends = ((me_f == 0).astype(jnp.int32), (me_f == fields - 1).astype(jnp.int32))
+
     barrier = pltpu.get_barrier_semaphore()
     for k in (1, banks - 1):
         pl.semaphore_signal(barrier, inc=1, device_id={"bank": bank_at[k]}, device_id_type=MESH)
-    for s in (0, 2):
-        pl.semaphore_signal(barrier, inc=1, device_id={"field": side_f[s]}, device_id_type=MESH)
+    for i in range(2):
+
+        @pl.when(has[i])
+        def _(i=i):
+            pl.semaphore_signal(barrier, inc=1, device_id={"field": side_f[2 * i]}, device_id_type=MESH)
+
+        @pl.when(jnp.logical_not(has[i]))
+        def _(i=i):
+            k3[2 * i] = jnp.zeros((48, 512), BF)
+            for q in range(colours):
+                f1[q, i] = jnp.zeros(f1.shape[2:], BF)
+                rs[q, 2 * i] = jnp.zeros(rs.shape[2:], BF)
+                gn[q, i] = jnp.zeros(gn.shape[2:], BF)
+
     for k in range(1, caps):
         pl.semaphore_signal(barrier, inc=1, device_id={"cap": cap_at[k]}, device_id_type=MESH)
 
@@ -84,15 +99,23 @@
                 second = ref[1, q].astype(F32)
                 k3[1, at : at + ranks, 0:511] = jnp.where(uses_one[t], second, first).astype(BF)
 
-    pl.semaphore_wait(barrier, 2 + 2 + caps - 1)
+    pl.semaphore_wait(barrier, 2 + 2 + caps - 1 - ends[0] - ends[1])
     sends = []
+
+    def to_side(copies, i):
+        @pl.when(has[i])
+        def _():
+            for copy in copies:
+                copy.start()
+
+        sends.append((i, copies))
+
     for i, s in enumerate((0, 2)):
         copy = pltpu.make_async_remote_copy(
             src_ref=k3.at[1], dst_ref=k3.at[2 - s], send_sem=k_s.at[i], recv_sem=k_r.at[1 - i],
             device_id={"field": side_f[s]}, device_id_type=MESH,
         )
-        copy.start()
-        sends.append(copy)
+        to_side([copy], i)
     pl.semaphore_signal(seen, inc=1, device_id={"bank": bank_at[banks - 1]}, device_id_type=MESH)
 
     tiles = 2 * PW // TILE
@@ -110,10 +133,6 @@
 
     def taps(s):
         lines = k3[s].astype(F32)
-        if s == 0:
-            lines = lines * (me_f > 0).astype(F32)
-        if s == 2:
-            lines = lines * (me_f < fields - 1).astype(F32)
         kf[s, 0:24, 256:768] = pltpu.roll(lines[0:24], 1, 1)
         kf[s, 24:48, 0:512] = lines[24:48]
 
@@ -160,10 +179,12 @@
         )
 
     def side_wait(src, dst, i, send, recv):
-        pltpu.make_async_remote_copy(
-            src_ref=src, dst_ref=dst(i), send_sem=send(i), recv_sem=recv(i),
-            device_id={"field": side_f[2 * i]}, device_id_type=MESH,
-        ).wait_recv()
+        @pl.when(has[i])
+        def _():
+            pltpu.make_async_remote_copy(
+                src_ref=src, dst_ref=dst(i), send_sem=send(i), recv_sem=recv(i),
+                device_id={"field": side_f[2 * i]}, device_id_type=MESH,
+            ).wait_recv()
 
     taps(1)
     for q in range(colours):
@@ -185,8 +206,7 @@
         for i, s in enumerate((0, 2)):
             f1s[q, i] = image(q, s).astype(BF)
             copy = side_copy(f1s.at[q, i], lambda i: f1.at[q, i], i, lambda i: f1_s.at[q, i], lambda i: f1_r.at[q, i])
-            copy.start()
-            sends.append(copy)
+            to_side([copy], i)
 
     def mid_one(q):
         for i in range(2):
@@ -201,7 +221,7 @@
                 device_id={"bank": bank_at[k]}, device_id_type=MESH,
             )
             copy.start()
-            sends.append(copy)
+            sends.append((2, [copy]))
 
     def mid_two(q):
         total = own[q] - meas[q].astype(F32)
@@ -214,8 +234,7 @@
         rs[q, 1] = (keep * total).astype(BF)
         for i in range(2):
             copy = side_copy(rs.at[q, 1], lambda i: rs.at[q, 2 * i], i, lambda i: r_s.at[q, i], lambda i: r_r.at[q, i])
-            copy.start()
-            sends.append(copy)
+            to_side([copy], i)
 
     def residual_wait(q):
         for i in range(2):
@@ -288,20 +307,21 @@
                 device_id={"cap": cap_at[k]}, device_id_type=MESH,
             )
             copy.start()
-            sends.append(copy)
+            sends.append((2, [copy]))
 
     def backward_sides(q):
         residual_wait(q)
         backward(q, (0, 2))
         for i in range(2):
+            copies = []
             for k in range(caps):
                 copy = pltpu.make_async_remote_copy(
                     src_ref=gs.at[q, i], dst_ref=gn.at[q, 1 - i, me_c],
                     send_sem=g_s.at[q, i, k], recv_sem=g_r.at[q, 1 - i, (caps - k) % caps],
                     device_id={"field": side_f[2 * i], "cap": cap_at[k]}, device_id_type=MESH,
                 )
-                copy.start()
-                sends.append(copy)
+                copies.append(copy)
+            to_side(copies, i)
 
     one = [jnp.where(u, 1.0, 0.0) for u in uses_one]
 
@@ -312,11 +332,16 @@
                 device_id={"cap": cap_at[k]}, device_id_type=MESH,
             ).wait_recv()
         for i in range(2):
-            for k in range(caps):
-                pltpu.make_async_remote_copy(
-                    src_ref=gs.at[q, i], dst_ref=gn.at[q, i, cap_at[k]], send_sem=g_s.at[q, i, k], recv_sem=g_r.at[q, i, k],
-                    device_id={"field": side_f[2 * i], "cap": cap_at[k]}, device_id_type=MESH,
-                ).wait_recv()
+
+            @pl.when(has[i])
+            def _(i=i):
+                for k in range(caps):
+                    pltpu.make_async_remote_copy(
+                        src_ref=gs.at[q, i], dst_ref=gn.at[q, i, cap_at[k]],
+                        send_sem=g_s.at[q, i, k], recv_sem=g_r.at[q, i, k],
+                        device_id={"field": side_f[2 * i], "cap": cap_at[k]}, device_id_type=MESH,
+                    ).wait_recv()
+
         total = ga[q, 0]
         for c in range(1, caps):
             total = total + ga[q, c]
@@ -350,8 +375,17 @@
     tail(0)
     tail(1)
     tail(2)
-    for copy in sends:
-        copy.wait_send()
+    for i in range(3):
+        mine = [copy for to, copies in sends for copy in copies if to == i]
+        if i == 2:
+            for copy in mine:
+                copy.wait_send()
+        else:
+
+            @pl.when(has[i])
+            def _(mine=mine):
+                for copy in mine:
+                    copy.wait_send()
 
 
 def body(pattern, measured, row_kernels, col_kernels, tile_patch, sat_tiles):

time: 48 us -> 43 us (0.90)
  the two profiles are of different devices: /device:TPU:1 before, /device:TPU:7 now
where the time goes in v4:
time: 43 us; the launch traced here: 42.8 us
  Pallas kernels  40.1 us (93%)
  local copies, waits for them, and re-layouts  2.06 us (5%)
  between operations  0.65 us (2%)
    pallas_call x1, Pallas kernels, body(): pl.pallas_call(functools.partial(kernel, fields, banks, caps, across), ou...  40.1 us
    unnamed x4, local copies, waits for them, and re-layouts  2.06 us

profile of v4, /device:TPU:7, one launch (start us, length us, event | category | flops | bytes accessed | tf_op | source)
XLA Modules:
  0.0 42.8 jit_solution(11550191089309086421)
XLA Ops:
  0.6 40.1 %shard_map.77 = (f32[2,3,4,511]{3,2,1,0:T(4,128)}, f32[2,3,4,511]{3,2,1,0:T(4,128)}) custom-call(s32[2]{0:T(128)} %tile_hbm.1, s32[1,256]{1,0:T(1,128)} %sat_hbm.1, bf16[1,3,32,256]{3,2,1,0:T(8,128)(2,1)} %meas_hbm.1, bf16[2,3,4,511]{3,2,1,0:T(4,128)(2,1)} %rowk_hbm.1, bf16[2,3,4,511]{3,2,1,0:T(4,128)(2,1)} %colk_hbm.1, bf16[1,3,542,256]{3,2,1,0:T(8,128)(2,1)} %pat_hbm.1), custom_call_target="tpu_custom_call" | custom-call | tf_op jit(solution)/shard_map/pallas_call | solution.py:399
  40.8 0.0 copy-start
  40.8 1.4 %copy.10 = f32[2,3,4,511]{3,2,1,0:T(4,128)} copy(f32[2,3,4,511]{3,2,1,0:T(4,128)} %get-tuple-element.4) | data formatting | bytes 98112
  42.2 0.0 copy-done
  42.2 0.6 %copy.11 = f32[2,3,4,511]{3,2,1,0:T(4,128)} copy(f32[2,3,4,511]{3,2,1,0:T(4,128)S(1)} %copy-done) | data formatting | bytes 98112
Async XLA Ops:
  40.8 1.4 %copy-start = (f32[2,3,4,511]{3,2,1,0:T(4,128)S(1)}, f32[2,3,4,511]{3,2,1,0:T(4,128)}, u32[]{:S(2)}) copy-start(f32[2,3,4,511]{3,2,1,0:T(4,128)} %get-tuple-element.5) | copy-start | bytes 147172
